TPU v7x, 512 devices: a whole 4x4x16 slice. The times are simulated.
512 devices in a mesh: dp: 32 (over z, y_lo), fsdp: 16 (over x, y_hi, core).
Axes of the slice: x: 4, y: 4 (y_hi: 2, y_lo: 2; y = y_hi * 2 + y_lo), z: 16, core: 2. Of those that a mesh axis runs over, the one named last changes fastest.
Arguments:
- hidden: bfloat16 [8192, 2048], P('dp', 'fsdp'), may hold values from -6 to 6
- upstream: bfloat16 [8192, 16384], P('dp', 'fsdp'), may hold values from -6 to 6
- rewards: float32 [256], P('dp'), may hold values from -4 to 4
- groups: int32 [256], P('dp'), may hold values from 0 to 63, as said below
- lengths: int32 [256], P('dp'), may hold values from 1 to 32, 6144 in all
- frozen_projection_weight: bfloat16 [2048, 16384], P('dp', 'fsdp'), may hold values from -0.125 to 0.125
- adapter_down_factor: float32 [256, 2048], P('dp', 'fsdp'), may hold values from -0.125 to 0.125
- adapter_up_factor: float32 [256, 16384], P('dp', 'fsdp'), may hold values from -0.01953125 to 0.01953125
- down_first_moment: float32 [256, 2048], P('dp', 'fsdp'), may hold values from -48.87522 to 48.87522
- down_second_moment: float32 [256, 2048], P('dp', 'fsdp'), may hold values from 0.8912896 to 8.912896
- up_first_moment: float32 [256, 16384], P('dp', 'fsdp'), may hold values from -122.18805 to 122.18805
- up_second_moment: float32 [256, 16384], P('dp', 'fsdp'), may hold values from 5.48864 to 54.8864
Outputs:
- hidden_input_gradient: bfloat16 [8192, 2048], P('dp', 'fsdp')
- fresh_down_factor: float32 [256, 2048], P('dp', 'fsdp')
- fresh_up_factor: float32 [256, 16384], P('dp', 'fsdp')
- fresh_down_first_moment: float32 [256, 2048], P('dp', 'fsdp')
- fresh_down_second_moment: float32 [256, 2048], P('dp', 'fsdp')
- fresh_up_first_moment: float32 [256, 16384], P('dp', 'fsdp')
- fresh_up_second_moment: float32 [256, 16384], P('dp', 'fsdp')
- sampler_merged_weight: bfloat16 [2048, 16384], P(None, 'fsdp')
Inputs may be any that keep to these rules, and one draw needn't show every extreme that they name: `groups`: each group holds exactly 4 completions, and all completions of a group lie in one aligned block of 8 completions.
All inputs are finite; a program needn't handle non-finite values. No bound on the sum of `lengths` on one device may be relied on, other than what follows from the above.
Results may differ from a plain program's by a relative error of at most 0.0051.
Values may be sent and summed in bfloat16 or wider, within the bound.
A program may use at most 64 MiB of HBM per device.

v0:
```python
import jax
import jax.numpy as jnp
from jax import lax
from jax.sharding import PartitionSpec as P

GROUP = 4
LEN = 32


adapter_scale = 2.0
learn_rate = 0.003
beta_one = 0.9
beta_two = 0.999
corr_one = 1.0 - 0.9**10
corr_two = 1.0 - 0.999**10
adam_eps = 1e-08


def contract_product(left, right, left_dim, right_dim):
    return lax.dot_general(
        left, right, (((left_dim,), (right_dim,)), ((), ())), preferred_element_type=jnp.float32
    )


def optimizer_update(param, grad, mean, var):
    next_mean = beta_one * mean + (1.0 - beta_one) * grad
    next_var = beta_two * var + (1.0 - beta_two) * grad * grad
    update = next_mean / corr_one / (jnp.sqrt(next_var / corr_two) + adam_eps)
    return (param - learn_rate * update, next_mean, next_var)


def body(
    hidden,
    upstream,
    rewards,
    groups,
    lengths,
    frozen_projection_weight,
    adapter_down_factor,
    adapter_up_factor,
    down_first_moment,
    down_second_moment,
    up_first_moment,
    up_second_moment,
):
    same = groups[:, None] == groups[None, :]
    group_mean = jnp.sum(jnp.where(same, rewards[None, :], jnp.float32(0.0)), axis=1) / GROUP
    advantage = rewards - group_mean
    positions = jnp.arange(LEN, dtype=jnp.int32)
    valid = positions[None, :] < lengths[:, None]
    weight = jnp.where(valid, -advantage[:, None], jnp.float32(0.0)).reshape(hidden.shape[0])
    output_gradient = (weight[:, None] * upstream.astype(jnp.float32)).astype(jnp.bfloat16)
    down_factor_columns, up_cols = (
        lax.all_gather(adapter_down_factor.astype(jnp.bfloat16), "dp", axis=0, tiled=True),
        lax.all_gather(adapter_up_factor.astype(jnp.bfloat16), "dp", axis=0, tiled=True),
    )
    in_part = contract_product(hidden, down_factor_columns, 1, 1)
    out_part = contract_product(output_gradient, up_cols, 1, 1)
    in_total, out_total = lax.psum((in_part, out_part), "fsdp")
    reduced_input = in_total.astype(jnp.bfloat16)
    reduced_output = out_total.astype(jnp.bfloat16)
    up_contribution = adapter_scale * contract_product(reduced_input, output_gradient, 0, 0)
    down_contribution = adapter_scale * contract_product(reduced_output, hidden, 0, 0)
    down_factor_gradient, up_factor_gradient = (
        lax.psum_scatter(down_contribution, "dp", scatter_dimension=0, tiled=True),
        lax.psum_scatter(up_contribution, "dp", scatter_dimension=0, tiled=True),
    )
    fresh_down_factor, fresh_down_first_moment, fresh_down_second_moment = optimizer_update(
        adapter_down_factor, down_factor_gradient, down_first_moment, down_second_moment
    )
    fresh_up_factor, fresh_up_first_moment, fresh_up_second_moment = optimizer_update(
        adapter_up_factor, up_factor_gradient, up_first_moment, up_second_moment
    )
    new_down_cols, new_up_cols = (
        lax.all_gather(fresh_down_factor.astype(jnp.bfloat16), "dp", axis=0, tiled=True),
        lax.all_gather(fresh_up_factor.astype(jnp.bfloat16), "dp", axis=0, tiled=True),
    )
    new_down_all = lax.all_gather(new_down_cols, "fsdp", axis=1, tiled=True)
    adapter_input = adapter_scale * contract_product(reduced_output, down_factor_columns, 1, 0)
    partial_value = contract_product(
        output_gradient, lax.all_gather(frozen_projection_weight, "dp", axis=0, tiled=True), 1, 1
    )
    own_rows = frozen_projection_weight.shape[0]
    first_row = lax.axis_index("dp") * own_rows
    own_down = lax.dynamic_slice_in_dim(new_down_all, first_row, own_rows, 1)
    local_weight_delta = contract_product(own_down, new_up_cols, 0, 0)
    local_merged_weight = (
        frozen_projection_weight.astype(jnp.float32) + adapter_scale * local_weight_delta
    ).astype(jnp.bfloat16)
    sampler_merged_weight = lax.all_gather(local_merged_weight, "dp", axis=0, tiled=True)
    frozen_output_sum = lax.psum_scatter(partial_value, "fsdp", scatter_dimension=1, tiled=True)
    hidden_input_gradient = (frozen_output_sum + adapter_input).astype(jnp.bfloat16)
    return (
        hidden_input_gradient,
        fresh_down_factor,
        fresh_up_factor,
        fresh_down_first_moment,
        fresh_down_second_moment,
        fresh_up_first_moment,
        fresh_up_second_moment,
        sampler_merged_weight,
    )


def solution(mesh):
    in_specs = (
        P("dp", "fsdp"),
        P("dp", "fsdp"),
        P("dp"),
        P("dp"),
        P("dp"),
        P("dp", "fsdp"),
        P("dp", "fsdp"),
        P("dp", "fsdp"),
        P("dp", "fsdp"),
        P("dp", "fsdp"),
        P("dp", "fsdp"),
        P("dp", "fsdp"),
    )
    out_specs = (
        P("dp", "fsdp"),
        P("dp", "fsdp"),
        P("dp", "fsdp"),
        P("dp", "fsdp"),
        P("dp", "fsdp"),
        P("dp", "fsdp"),
        P("dp", "fsdp"),
        P(None, "fsdp"),
    )
    return jax.shard_map(body, mesh=mesh, in_specs=in_specs, out_specs=out_specs, check_vma=False)
```

profile of v0, /device:TPU:1, one launch (start us, length us, event | category | flops | bytes accessed | tf_op | source)
XLA Modules:
  0.0 1049.7 jit_solution(1450611198943325453)
XLA Ops:
  7.3 0.9 select_reduce_fusion
  9.6 0.7 fusion.10
  10.4 0.8 convert_element_type.35
  11.2 56.1 %all_gather.23 = bf16[256,128]{1,0:T(8,128)(2,1)S(1)} all-gather(bf16[8,128]{1,0:T(8,128)(2,1)S(1)} %convert_element_type.37), channel_id=1, replica_groups=mesh['dp'=32,'fsdp'=16] {'dp'}, dimensions={0}, use_global_device_ids=true | all-gather | bytes 67584 | tf_op jit(solution)/shard_map/all_gather | solution.py:54
  67.5 47.6 %all_gather.22 = bf16[256,1024]{1,0:T(8,128)(2,1)S(1)} all-gather(bf16[8,1024]{1,0:T(8,128)(2,1)S(1)} %convert_element_type.35), channel_id=1, replica_groups=mesh['dp'=32,'fsdp'=16] {'dp'}, dimensions={0}, use_global_device_ids=true | all-gather | bytes 540672 | tf_op jit(solution)/shard_map/all_gather | solution.py:55
  115.1 1.4 fusion.12
  116.5 92.5 %all-reduce.6 = (bf16[256,256]{1,0:T(8,128)(2,1)S(1)}, bf16[256,256]{1,0:T(8,128)(2,1)S(1)}) all-reduce(f32[256,256]{1,0:T(8,128)S(1)} %fusion.12, f32[256,256]{1,0:T(8,128)S(1)} %fusion.18), channel_id=1, replica_groups=mesh['dp'=32,'fsdp'=16] {'fsdp'}, use_global_device_ids=true, to_apply=%region_2.3 | all-reduce | flops 131072 | bytes 786432 | tf_op jit(solution)/shard_map/psum | solution.py:59
  209.0 0.9 convolution_multiply_fusion.2
  210.0 2.4 convolution_multiply_fusion
  212.5 1.3 dynamic-slice
  214.4 226.8 %all-reduce.5.cloned.1.call-done = f32[256,128]{1,0:T(8,128)} async-done(((f32[256,128]{1,0:T(8,128)}), f32[256,128]{1,0:T(8,128)}) %all-reduce.5.cloned.1.call-update) | async-done | bytes 131088
  441.2 1.3 fusion.14
  442.5 51.6 %all_gather.24 = bf16[256,128]{1,0:T(8,128)(2,1)} all-gather(bf16[8,128]{1,0:T(8,128)(2,1)S(1)} %get-tuple-element.10), channel_id=1, replica_groups=mesh['dp'=32,'fsdp'=16] {'dp'}, dimensions={0}, use_global_device_ids=true | all-gather | bytes 67584 | tf_op jit(solution)/shard_map/all_gather | solution.py:75
  494.8 80.8 %reduce-scatter.5.cloned.1.call-done = f32[8,1024]{1,0:T(8,128)} async-done(((f32[256,1024]{1,0:T(8,128)}), f32[8,1024]{1,0:T(8,128)}) %reduce-scatter.5.cloned.1.call-update) | async-done | bytes 32784 | tf_op jit(solution)/shard_map/reduce_scatter | solution.py:66
  575.5 1.4 fusion.16
  576.9 48.2 %all_gather.26 = bf16[256,1024]{1,0:T(8,128)(2,1)S(1)} all-gather(bf16[8,1024]{1,0:T(8,128)(2,1)S(1)} %get-tuple-element.14), channel_id=1, replica_groups=mesh['dp'=32,'fsdp'=16] {'dp'}, dimensions={0}, use_global_device_ids=true | all-gather | bytes 540672 | tf_op jit(solution)/shard_map/all_gather | solution.py:76
  625.2 36.6 %all-gather.6.cloned.1.call-done = bf16[256,2048]{1,0:T(8,128)(2,1)} async-done(((bf16[256,128]{1,0:T(8,128)(2,1)}), bf16[256,2048]{1,0:T(8,128)(2,1)}) %all-gather.6.cloned.1.call-update) | async-done | bytes 1048592 | tf_op jit(solution)/shard_map/all_gather | solution.py:78
  661.8 1.8 fusion.1
  663.6 119.4 %all-gather.4.cloned.1.call-done = bf16[2048,1024]{1,0:T(8,128)(2,1)} async-done(((bf16[64,1024]{1,0:T(8,128)(2,1)}), bf16[2048,1024]{1,0:T(8,128)(2,1)}) %all-gather.4.cloned.1.call-update) | async-done | bytes 4194320 | tf_op jit(solution)/shard_map/all_gather | solution.py:81
  783.1 4.8 fusion.13
  788.0 135.1 %all-gather.8.cloned.1.call-done = bf16[2048,1024]{1,0:T(8,128)(2,1)} async-done(((bf16[64,1024]{1,0:T(8,128)(2,1)}), bf16[2048,1024]{1,0:T(8,128)(2,1)}) %all-gather.8.cloned.1.call-update) | async-done | bytes 4194320 | tf_op jit(solution)/shard_map/all_gather | solution.py:90
  923.1 113.4 %reduce-scatter.3.cloned.1.call-done = f32[256,128]{1,0:T(8,128)} async-done(((f32[256,2048]{1,0:T(8,128)}), f32[256,128]{1,0:T(8,128)}) %reduce-scatter.3.cloned.1.call-update) | async-done | bytes 131088 | tf_op jit(solution)/shard_map/reduce_scatter | solution.py:91
  1036.5 1.7 fusion.3
  1038.2 4.6 copy.26
  (34 shorter events, 2.5 us)
Async XLA Ops:
  7.2 60.1 %copy-start = (bf16[256,128]{1,0:T(8,128)(2,1)S(1)}, bf16[256,128]{1,0:T(8,128)(2,1)}, u32[]{:S(2)}) copy-start(bf16[256,128]{1,0:T(8,128)(2,1)} %param.12) | copy-start | bytes 196612
  7.2 434.0 %copy-start.6 = (f32[8,128]{1,0:T(8,128)S(1)}, f32[8,128]{1,0:T(8,128)}, u32[]{:S(2)}) copy-start(f32[8,128]{1,0:T(8,128)} %param.18) | copy-start | bytes 12292
  7.2 568.3 %copy-start.3 = (f32[8,1024]{1,0:T(8,128)S(1)}, f32[8,1024]{1,0:T(8,128)}, u32[]{:S(2)}) copy-start(f32[8,1024]{1,0:T(8,128)} %param.19) | copy-start | bytes 98308
  7.2 775.9 %copy-start.1 = (bf16[256,1024]{1,0:T(8,128)(2,1)S(1)}, bf16[256,1024]{1,0:T(8,128)(2,1)}, u32[]{:S(2)}) copy-start(bf16[256,1024]{1,0:T(8,128)(2,1)} %param.13) | copy-start | bytes 1572868
  7.2 434.0 %copy-start.8 = (f32[8,128]{1,0:T(8,128)S(1)}, f32[8,128]{1,0:T(8,128)}, u32[]{:S(2)}) copy-start(f32[8,128]{1,0:T(8,128)} %param.21) | copy-start | bytes 12292
  7.2 434.0 %copy-start.7 = (f32[8,128]{1,0:T(8,128)S(1)}, f32[8,128]{1,0:T(8,128)}, u32[]{:S(2)}) copy-start(f32[8,128]{1,0:T(8,128)} %param.20) | copy-start | bytes 12292
  7.2 654.5 %copy-start.2 = (bf16[64,1024]{1,0:T(8,128)(2,1)S(1)}, bf16[64,1024]{1,0:T(8,128)(2,1)}, u32[]{:S(2)}) copy-start(bf16[64,1024]{1,0:T(8,128)(2,1)} %param.17) | copy-start | bytes 393220
  7.3 568.3 %copy-start.5 = (f32[8,1024]{1,0:T(8,128)S(1)}, f32[8,1024]{1,0:T(8,128)}, u32[]{:S(2)}) copy-start(f32[8,1024]{1,0:T(8,128)} %param.23) | copy-start | bytes 98308
  7.3 568.3 %copy-start.4 = (f32[8,1024]{1,0:T(8,128)S(1)}, f32[8,1024]{1,0:T(8,128)}, u32[]{:S(2)}) copy-start(f32[8,1024]{1,0:T(8,128)} %param.22) | copy-start | bytes 98308
  7.3 433.9 %all-reduce.5.cloned.1.call-start = ((), (), s32[]{:S(2)}) async-start(), calls=%async_computation.7 | async-start | bytes 262144
  209.9 365.6 %reduce-scatter.5.cloned.1.call-start = ((), (), s32[]{:S(2)}) async-start(), calls=%async_computation.4 | async-start | bytes 1081344 | tf_op jit(solution)/shard_map/reduce_scatter | solution.py:66
  212.4 449.4 %all-gather.6.cloned.1.call-start = ((), (), s32[]{:S(2)}) async-start(), calls=%async_computation.5 | async-start | bytes 1114112 | tf_op jit(solution)/shard_map/all_gather | solution.py:78
  494.1 288.9 %all-gather.4.cloned.1.call-start = ((), (), s32[]{:S(2)}) async-start(), calls=%async_computation.2 | async-start | bytes 4325376 | tf_op jit(solution)/shard_map/all_gather | solution.py:81
  494.7 428.4 %all-gather.8.cloned.1.call-start = ((), (), s32[]{:S(2)}) async-start(), calls=%async_computation.6 | async-start | bytes 4325376 | tf_op jit(solution)/shard_map/all_gather | solution.py:90
  663.6 372.9 %reduce-scatter.3.cloned.1.call-start = ((), (), s32[]{:S(2)}) async-start(), calls=%async_computation.3 | async-start | bytes 2228224 | tf_op jit(solution)/shard_map/reduce_scatter | solution.py:91
Sparse Core Ops, SparseCore 0:
  210.0 231.1 all-reduce.4
  444.8 130.6 reduce-scatter.4
  578.7 83.0 all-gather.5
  663.7 119.3 all-gather.3
  785.0 138.0 all-gather.7
  928.3 108.1 reduce-scatter.2
where the time goes:
time: 1050 us
  waiting for transfers between devices  713 us (68%)
  blocking collectives  296 us (28%)
  between operations  14.9 us (1%)
  matrix products  13.2 us (1%)
    unnamed x7, waiting for transfers between devices  227 us
    all_gather x1, waiting for transfers between devices, body(): lax.all_gather(local_merged_weight, 'dp', axis=0, tiled=True)  135 us
    all_gather x1, waiting for transfers between devices, body(): lax.all_gather(frozen_projection_weight, 'dp', axis=0, tiled=True)  119 us
    reduce_scatter x1, waiting for transfers between devices, body(): lax.psum_scatter(partial_value, 'fsdp', scatter_dimension=1, tiled=True)  113 us
    psum x1, blocking collectives, body(): in_total, out_total = lax.psum((in_part, out_part), 'fsdp')  92.5 us
    reduce_scatter x1, waiting for transfers between devices, body(): lax.psum_scatter(up_contribution, 'dp', scatter_dimension=0, tiled=True)  80.8 us
    all_gather x1, blocking collectives, body(): lax.all_gather(adapter_down_factor.astype(jnp.bfloat16), 'dp', axis=0, ti...  56.1 us
    all_gather x1, blocking collectives, body(): lax.all_gather(fresh_down_factor.astype(jnp.bfloat16), 'dp', axis=0, tile...  51.6 us
  transfers between devices with their start and end apart: 6, of which 6 were waited for; matrix products, arithmetic and copies ran while one was open for 1% of the time, Pallas kernels for 0%

commit v1 on v0

v1 whole, which is shorter than its diff:
```python
import jax
import jax.numpy as jnp
from jax import lax
from jax.experimental import pallas as pl
from jax.experimental.pallas import tpu as pltpu
from jax.sharding import PartitionSpec as P

GROUP = 4
LEN = 32
MESH = pl.DeviceIdType.MESH

adapter_scale = 2.0
learn_rate = 0.003
beta_one = 0.9
beta_two = 0.999
corr_one = 1.0 - 0.9**10
corr_two = 1.0 - 0.999**10
adam_eps = 1e-08

bf16 = jnp.bfloat16
f32 = jnp.float32

Y_LO = (0, 1, 0, 0, 0)
Y_HI = (0, 0, 0, 1, 0)
CORE = (0, 0, 0, 0, 1)
FAR = tuple((dz, 0, 0, 0, 0) for dz in (8, 4, -4))
NEAR = tuple((dz, 0, 0, 0, 0) for dz in (2, 1, -1))
X_RING = tuple((0, 0, dx, 0, 0) for dx in (2, 1, -1))
X_CORE = tuple((0, 0, dx, 0, dc) for dx in (2, 1, -1, 0) for dc in (1, 0) if (dx, dc) != (0, 0))
PEERS = FAR + NEAR + (Y_LO, Y_HI) + X_CORE


def coords():
    dp = lax.axis_index("dp")
    fs = lax.axis_index("fsdp")
    return dp // 2, dp % 2, fs // 4, (fs // 2) % 2, fs % 2


def device(off):
    z, yl, x, yh, c = coords()
    z = (z + off[0] + 16) % 16
    yl = (yl + off[1]) % 2
    x = (x + off[2] + 4) % 4
    yh = (yh + off[3]) % 2
    c = (c + off[4]) % 2
    return (2 * z + yl, 4 * x + 2 * yh + c)


def inverse(off):
    return (-off[0], off[1], -off[2], off[3], off[4])


def dot(left, right, left_dim, right_dim):
    return lax.dot_general(
        left, right, (((left_dim,), (right_dim,)), ((), ())), preferred_element_type=f32
    )


def rows(start, size):
    return pl.ds(pl.multiple_of(start * size, size), size)


def adam(param, grad, mean, var):
    next_mean = beta_one * mean + (1.0 - beta_one) * grad
    next_var = beta_two * var + (1.0 - beta_two) * grad * grad
    update = next_mean / corr_one / (jnp.sqrt(next_var / corr_two) + adam_eps)
    return (param - learn_rate * update, next_mean, next_var)


def exchange_kernel(
    hid, ups, wt, w_own, dn, up, dm, dv, um, uv,
    w_all, nd, fu, hig, fdn, fup, fdm, fdv, fum, fuv,
    g, wb, pair, f, a, rx, sy, ty, low,
    cd, cu, nrd, nru, md, mu, frd, fru, yd, yu, yrd, yru, pd, pu, fd,
    pt, pr1, q, pr2, r, rb, pr3, send_sem, recv_sem, local_sem,
):
    z, yl, x, yh, c = coords()
    pos = (z % 4) * 4 + z // 4
    count = [0]
    sent = []

    def send(src, dst, off):
        i = count[0]
        assert i < 72
        count[0] += 1
        copy = pltpu.make_async_remote_copy(
            src_ref=src,
            dst_ref=dst,
            send_sem=send_sem.at[i],
            recv_sem=recv_sem.at[i],
            device_id=device(off),
            device_id_type=MESH,
        )
        copy.start()
        sent.append(copy)
        return copy

    def arrive(copies):
        for copy in copies:
            copy.wait_recv()

    def pair_send(buf):
        return send(buf.at[rows(yl, 8)], buf.at[rows(yl, 8)], Y_LO)

    def far_send(buf):
        mine = rows(pos, 16)
        return [send(buf.at[mine], buf.at[mine], off) for off in FAR]

    def near_send(buf):
        mine = rows(z % 4, 64)
        return [send(buf.at[mine], buf.at[mine], off) for off in NEAR]

    def near_parts(buf, slots):
        return [
            send(buf.at[rows((z + off[0] + 16) % 4, 64)], slots.at[i], off)
            for i, off in enumerate(NEAR)
        ]

    def near_sum(buf, slots):
        total = buf[rows(z % 4, 64), :].astype(f32)
        for i in range(3):
            total = total + slots[i].astype(f32)
        return total

    def far_parts(buf, slots):
        return [
            send(buf.at[rows(((z + off[0] + 16) % 16) // 4, 16)], slots.at[i], off)
            for i, off in enumerate(FAR)
        ]

    def far_sum(buf, slots):
        total = buf[rows(z // 4, 16), :].astype(f32)
        for i in range(3):
            total = total + slots[i].astype(f32)
        return total

    def pair_parts(buf, slot):
        return send(buf.at[rows(1 - yl, 8)], slot, Y_LO)

    def w_group(group):
        return wb.at[rows(group % 4, 4), rows(yl, 64), :]

    def w_block(zz):
        zz = (zz + 16) % 16
        return wb.at[(zz % 4) * 4 + zz // 4, rows(yl, 64), :]

    barrier = pltpu.get_barrier_semaphore()
    for off in PEERS:
        pl.semaphore_signal(barrier, inc=1, device_id=device(inverse(off)), device_id_type=MESH)
    pair[rows(yl, 8), 0:1024] = up[...]
    pair[rows(yl, 8), 1024:1152] = dn[...]
    wb[pos, rows(yl, 64), :] = w_own[...]
    pl.semaphore_wait(barrier, len(PEERS))

    s = pair_send(pair)
    g[...] = (wt[...] * ups[...].astype(f32)).astype(bf16)
    s.wait_recv()
    f[rows(pos, 16), :] = pair[...].astype(bf16)
    far = far_send(f)
    w_far = [send(w_block(z), w_block(z), FAR[1]), send(w_block(z), w_block(z), FAR[2])]
    arrive(far)
    near = near_send(f)
    arrive(near)

    a[0:256, :] = dot(f[:, 1024:1152], hid[...], 1, 1).astype(bf16)
    a[256:512, :] = dot(f[:, 0:1024], g[...], 1, 1).astype(bf16)
    j = 2 * x + c
    scattered = []
    for i, off in enumerate(X_CORE):
        to = 2 * ((x + off[2] + 4) % 4) + (c + off[4]) % 2
        scattered.append(send(a.at[rows(to, 64)], rx.at[i], off))
    arrive(w_far)
    w_far2 = send(w_block(z - 4), w_block(z - 4), FAR[1])
    arrive(scattered)
    total = a[rows(j, 64), :].astype(f32)
    for i in range(7):
        total = total + rx[i].astype(f32)
    sy[...] = total.astype(bf16)
    s = send(sy, ty, Y_HI)
    s.wait_recv()
    low[rows(j, 64), :] = (sy[...].astype(f32) + ty[...].astype(f32)).astype(bf16)
    gathered = [send(low.at[rows(j, 64)], low.at[rows(j, 64)], off) for off in X_CORE]
    w_far2.wait_recv()
    w_near = [send(w_group(z), w_group(z), NEAR[1]), send(w_group(z), w_group(z), NEAR[2])]
    w_pair = [send(w_group(z), w_group(z), Y_LO)]
    arrive(gathered)

    cd[...] = (adapter_scale * dot(low[256:512, :], hid[...], 1, 0)).astype(bf16)
    near_d = near_parts(cd, nrd)
    cu[...] = (adapter_scale * dot(low[0:256, :], g[...], 1, 0)).astype(bf16)
    near_u = near_parts(cu, nru)
    arrive(near_d)
    md[...] = near_sum(cd, nrd).astype(bf16)
    far_d = far_parts(md, frd)
    arrive(near_u)
    mu[...] = near_sum(cu, nru).astype(bf16)
    far_u = far_parts(mu, fru)
    arrive(w_near)
    w_near2 = send(w_group(z + 1), w_group(z + 1), NEAR[2])
    w_pair.append(send(w_group(z + 1), w_group(z + 1), Y_LO))
    w_pair.append(send(w_group(z + 3), w_group(z + 3), Y_LO))
    arrive(far_d)
    yd[...] = far_sum(md, frd)
    s = pair_parts(yd, yrd)
    s.wait_recv()
    fdn[...], fdm[...], fdv[...] = adam(dn[...], yd[rows(yl, 8), :] + yrd[...], dm[...], dv[...])
    pd[rows(yl, 8), :] = fdn[...]
    s = pair_send(pd)
    arrive(far_u)
    yu[...] = far_sum(mu, fru)
    s_u = pair_parts(yu, yru)
    s.wait_recv()
    fd[rows(pos, 16), :] = pd[...].astype(bf16)
    far_d = far_send(fd)
    s_u.wait_recv()
    fup[...], fum[...], fuv[...] = adam(up[...], yu[rows(yl, 8), :] + yru[...], um[...], uv[...])
    pu[rows(yl, 8), :] = fup[...]
    s_u = pair_send(pu)
    w_near2.wait_recv()
    w_pair.append(send(w_group(z + 2), w_group(z + 2), Y_LO))
    s_u.wait_recv()
    fu[rows(pos, 16), :] = pu[...].astype(bf16)
    far_u = far_send(fu)
    arrive(far_d)
    near_d = near_send(fd)
    arrive(far_u)
    near_u = near_send(fu)
    arrive(near_d)

    k = 2 * x + yh
    nd[c, k] = fd[...]
    s = send(nd.at[c, k], nd.at[c, k], Y_HI)

    arrive(w_pair)
    w_copy = pltpu.make_async_copy(wb, w_all, local_sem)
    w_copy.start()

    def product(p, carry):
        group = p // 4
        pt[group % 2, 2 * (p % 4) + group // 2] = dot(wb[p], g[...], 1, 1).astype(bf16)
        return carry

    lax.fori_loop(0, 16, product, 0)
    s_p = send(pt.at[1 - c], pr1, CORE)
    s.wait_recv()
    spread = [send(nd.at[c, rows(x, 2)], nd.at[c, rows(x, 2)], off) for off in X_RING]
    s_p.wait_recv()

    def core_sum(i, carry):
        q[i] = (pt[c, i].astype(f32) + pr1[i].astype(f32)).astype(bf16)
        return carry

    lax.fori_loop(0, 8, core_sum, 0)
    x_parts = [
        send(q.at[rows((x + off[2] + 4) % 4, 2)], pr2.at[i], off) for i, off in enumerate(X_RING)
    ]
    arrive(spread)
    s = send(nd.at[c], nd.at[c], CORE)
    arrive(x_parts)
    total = q[rows(x, 2)].astype(f32)
    for i in range(3):
        total = total + pr2[i].astype(f32)
    r[...] = total
    rb[...] = r[1 - yh].astype(bf16)
    s_p = send(rb, pr3, Y_HI)
    own = adapter_scale * dot(low[256:512, :], f[:, 1024:1152], 0, 0)
    s_p.wait_recv()
    hig[...] = (jnp.transpose(r[yh] + pr3[...].astype(f32)) + own).astype(bf16)
    s.wait_recv()
    arrive(near_u)
    for copy in sent:
        copy.wait_send()
    w_copy.wait()


def exchange(*args):
    def out(shape, dtype):
        return jax.ShapeDtypeStruct(shape, dtype)

    vmem = pl.BlockSpec(memory_space=pltpu.VMEM)
    scratch = [
        ((256, 1024), bf16), ((16, 128, 1024), bf16), ((16, 1152), f32), ((256, 1152), bf16),
        ((512, 256), bf16), ((7, 64, 256), bf16), ((64, 256), bf16), ((64, 256), bf16),
        ((512, 256), bf16),
        ((256, 128), bf16), ((256, 1024), bf16), ((3, 64, 128), bf16), ((3, 64, 1024), bf16),
        ((64, 128), bf16), ((64, 1024), bf16), ((3, 16, 128), bf16), ((3, 16, 1024), bf16),
        ((16, 128), f32), ((16, 1024), f32), ((8, 128), f32), ((8, 1024), f32),
        ((16, 128), f32), ((16, 1024), f32), ((256, 128), bf16),
        ((2, 8, 128, 256), bf16), ((8, 128, 256), bf16), ((8, 128, 256), bf16),
        ((3, 2, 128, 256), bf16), ((2, 128, 256), f32), ((128, 256), bf16), ((128, 256), bf16),
    ]
    messages = 72
    return pl.pallas_call(
        exchange_kernel,
        name="exchange",
        out_shape=[
            out((16, 128, 1024), bf16),
            out((2, 8, 256, 128), bf16),
            out((256, 1024), bf16),
            out((256, 128), bf16),
            out((8, 128), f32),
            out((8, 1024), f32),
            out((8, 128), f32),
            out((8, 128), f32),
            out((8, 1024), f32),
            out((8, 1024), f32),
        ],
        in_specs=[vmem] * 10,
        out_specs=[pl.BlockSpec(memory_space=pl.ANY)] + [vmem] * 9,
        scratch_shapes=[pltpu.VMEM(shape, dtype) for shape, dtype in scratch]
        + [
            pltpu.SemaphoreType.DMA((messages,)),
            pltpu.SemaphoreType.DMA((messages,)),
            pltpu.SemaphoreType.DMA,
        ],
        compiler_params=pltpu.CompilerParams(
            collective_id=0, has_side_effects=True, vmem_limit_bytes=40 << 20
        ),
    )(*args)


def merge_kernel(w, nd, fu, *refs):
    merged = refs[-1]
    merged[...] = (
        w[0].astype(f32) + adapter_scale * dot(nd[0, 0], fu[...], 0, 0)
    ).astype(bf16)

    @pl.when(pl.program_id(0) == 0)
    def _():
        for i in range(7):
            refs[7 + i][...] = refs[i][...]


def merge(w, nd, fu, *rest):
    def whole(array):
        return pl.BlockSpec(array.shape, lambda i: (0,) * len(array.shape))

    return pl.pallas_call(
        merge_kernel,
        name="merge",
        grid=(16,),
        in_specs=[
            pl.BlockSpec((1, 128, 1024), lambda i: ((i % 4) * 4 + i // 4, 0, 0)),
            pl.BlockSpec((1, 1, 256, 128), lambda i: (i % 2, 2 * (i // 4) + (i // 2) % 2, 0, 0)),
            whole(fu),
        ]
        + [whole(array) for array in rest],
        out_specs=[whole(array) for array in rest]
        + [pl.BlockSpec((128, 1024), lambda i: (i, 0))],
        out_shape=[jax.ShapeDtypeStruct(array.shape, array.dtype) for array in rest]
        + [jax.ShapeDtypeStruct((2048, 1024), bf16)],
        compiler_params=pltpu.CompilerParams(vmem_limit_bytes=40 << 20),
    )(w, nd, fu, *rest)


def body(
    hidden,
    upstream,
    rewards,
    groups,
    lengths,
    frozen_projection_weight,
    adapter_down_factor,
    adapter_up_factor,
    down_first_moment,
    down_second_moment,
    up_first_moment,
    up_second_moment,
):
    same = groups[:, None] == groups[None, :]
    group_mean = jnp.sum(jnp.where(same, rewards[None, :], jnp.float32(0.0)), axis=1) / GROUP
    advantage = rewards - group_mean
    positions = jnp.arange(LEN, dtype=jnp.int32)
    valid = positions[None, :] < lengths[:, None]
    weight = jnp.where(valid, -advantage[:, None], jnp.float32(0.0)).reshape(hidden.shape[0], 1)
    w_all, nd, fu, *rest = exchange(
        hidden,
        upstream,
        weight,
        frozen_projection_weight,
        adapter_down_factor,
        adapter_up_factor,
        down_first_moment,
        down_second_moment,
        up_first_moment,
        up_second_moment,
    )
    return tuple(merge(w_all, nd, fu, *rest))


def solution(mesh):
    split = P("dp", "fsdp")
    in_specs = (split, split, P("dp"), P("dp"), P("dp")) + (split,) * 7
    out_specs = (split,) * 7 + (P(None, "fsdp"),)
    return jax.shard_map(body, mesh=mesh, in_specs=in_specs, out_specs=out_specs, check_vma=False)
```

time: 1050 us -> 169 us (0.16)
  waiting for transfers between devices: 713 us -> 0 us
  blocking collectives: 296 us -> 0 us
  Pallas kernels: 0 us -> 158 us
  between operations: 14.9 us -> 0.67 us
  matrix products: 13.2 us -> 0 us
    all_gather x3 -> x0, waiting for transfers between devices: 291 us -> none  [the longest x1 135 us: body(): lax.all_gather(local_merged_weight, 'dp', axis=0, tiled=True)]
    unnamed x7 -> x0, waiting for transfers between devices: 227 us -> none
    all_gather x4 -> x0, blocking collectives: 204 us -> none  [the longest x1 56.1 us: body(): lax.all_gather(adapter_down_factor.astype(jnp.bfloat16), 'dp', axis=0, ti...]
    reduce_scatter x2 -> x0, waiting for transfers between devices: 194 us -> none  [the longest x1 113 us: body(): lax.psum_scatter(partial_value, 'fsdp', scatter_dimension=1, tiled=True)]
    pallas_call x0 -> x2, Pallas kernels: none -> 158 us  [the longest x1 149 us: exchange(): pl.pallas_call(exchange_kernel, name='exchange', out_shape=[out((16, 128,...]
    psum x1 -> x0, blocking collectives: 92.5 us -> none  [body(): in_total, out_total = lax.psum((in_part, out_part), 'fsdp')]
    dot_general x7 -> x0, matrix products: 13.2 us -> none  [contract_product(): lax.dot_general(left, right, (((left_dim,), (right_dim,)), ((), ())), pre...]
  transfers between devices with their start and end apart: 6 -> 0, of which waited for: 6 -> 0; matrix products, arithmetic and copies ran while one was open for 1% -> 0% of each run, Pallas kernels for 0% -> 0%
where the time goes in v1:
time: 169 us; the launch traced here: 168 us
  Pallas kernels  158 us (93%)
  local copies, waits for them, and re-layouts  7.24 us (4%)
  other arithmetic  2.3 us (1%)
    pallas_call x1, Pallas kernels, exchange(): pl.pallas_call(exchange_kernel, name='exchange', out_shape=[out((16, 128,...  149 us
    pallas_call x1, Pallas kernels, merge(): pl.pallas_call(merge_kernel, name='merge', grid=(16,), in_specs=[pl.Block...  8.27 us
    unnamed x18, local copies, waits for them, and re-layouts  7.11 us

profile of v1, /device:TPU:1, one launch (start us, length us, event | category | flops | bytes accessed | tf_op | source)
XLA Modules:
  0.0 168.0 jit_solution(6473419027622321629)
XLA Ops:
  0.6 0.9 select_reduce_fusion
  1.5 0.7 subtract_negate_fusion
  2.2 0.7 fusion
  2.9 0.1 select_n.21.wt
  3.1 0.0 copy-start
  3.1 1.0 copy-done
  4.1 0.0 copy-start.1
  4.1 0.9 copy-done.1
  5.0 0.0 copy-start.2
  5.0 0.8 copy-done.2
  5.9 0.0 copy-start.3
  5.9 0.8 copy-done.3
  6.6 0.0 copy-start.4
  6.6 0.8 copy-done.4
  7.4 0.0 copy-start.5
  7.4 0.8 copy-done.5
  8.1 0.0 copy-start.6
  8.1 0.7 copy-done.6
  8.8 0.0 copy-start.7
  8.8 0.7 copy-done.7
  9.5 0.0 copy-start.8
  9.5 0.7 copy-done.8
  10.2 149.5 %exchange.1 = (bf16[16,128,1024]{2,1,0:T(8,128)(2,1)S(1)}, bf16[2,8,256,128]{3,2,1,0:T(8,128)(2,1)S(1)}, bf16[256,1024]{1,0:T(8,128)(2,1)S(1)}, bf16[256,128]{1,...) custom-call(bf16[256,128]{1,0:T(8,128)(2,1)S(1)} %copy-done.2, ...), custom_call_target="tpu_custom_call" | custom-call | tf_op jit(solution)/shard_map/exchange/pallas_call | solution.py:293
  159.7 8.3 %merge.1 = (bf16[256,128]{1,0:T(8,128)(2,1)}, f32[8,128]{1,0:T(8,128)}, f32[8,1024]{1,0:T(8,128)}, f32[8,128]{1,0:T(8,128)}, f32[8,128]{1,0:T(8,128)}, /*index=5...) custom-call(bf16[16,128,1024]{2,1,0:T(8,128)(2,1)S(1)} %get-tuple-element.18.w, ...), custom_call_target="tpu_custom_call" | custom-call | tf_op jit(solution)/shard_map/merge/pallas_call | solution.py:338
Async XLA Ops:
  3.1 1.0 copy-start
  4.1 0.9 copy-start.1
  5.0 0.8 copy-start.2
  5.9 0.8 copy-start.3
  6.6 0.8 copy-start.4
  7.4 0.8 copy-start.5
  8.1 0.7 copy-start.6
  8.8 0.7 copy-start.7
  9.5 0.7 copy-start.8

commit v2 on v1

v2 whole, which is shorter than its diff:
```python
import jax
import jax.numpy as jnp
from jax import lax
from jax.experimental import pallas as pl
from jax.experimental.pallas import tpu as pltpu
from jax.sharding import PartitionSpec as P

GROUP = 4
LEN = 32
MESH = pl.DeviceIdType.MESH

adapter_scale = 2.0
learn_rate = 0.003
beta_one = 0.9
beta_two = 0.999
corr_one = 1.0 - 0.9**10
corr_two = 1.0 - 0.999**10
adam_eps = 1e-08

bf16 = jnp.bfloat16
f32 = jnp.float32

Y_LO = (0, 1, 0, 0, 0)
Y_HI = (0, 0, 0, 1, 0)
CORE = (0, 0, 0, 0, 1)
FAR = tuple((dz, dy, 0, 0, 0) for dz, dy in ((4, 0), (-4, 1), (4, 1), (-4, 0), (0, 1)))
PLUS4, MINUS4_ACROSS, _, MINUS4, _ = FAR
NEAR = tuple((dz, 0, 0, 0, 0) for dz in (2, -2, 1, -1))
PLUS2, MINUS2, PLUS1, MINUS1 = NEAR
X_RING = tuple((0, 0, dx, 0, 0) for dx in (2, 1, -1))
X_CORE = tuple((0, 0, dx, 0, dc) for dx in (2, 1, -1, 0) for dc in (1, 0) if (dx, dc) != (0, 0))
PEERS = FAR + NEAR + (Y_HI,) + X_CORE
MESSAGES = 128


def coords():
    dp = lax.axis_index("dp")
    fs = lax.axis_index("fsdp")
    return dp // 2, dp % 2, fs // 4, (fs // 2) % 2, fs % 2


def device(off):
    z, yl, x, yh, c = coords()
    z = (z + off[0] + 16) % 16
    yl = (yl + off[1]) % 2
    x = (x + off[2] + 4) % 4
    yh = (yh + off[3]) % 2
    c = (c + off[4]) % 2
    return (2 * z + yl, 4 * x + 2 * yh + c)


def inverse(off):
    return (-off[0], off[1], -off[2], off[3], off[4])


def dot(left, right, left_dim, right_dim):
    return lax.dot_general(
        left, right, (((left_dim,), (right_dim,)), ((), ())), preferred_element_type=f32
    )


def rows(start, size):
    return pl.ds(pl.multiple_of(start * size, size), size)


def adam(param, grad, mean, var):
    next_mean = beta_one * mean + (1.0 - beta_one) * grad
    next_var = beta_two * var + (1.0 - beta_two) * grad * grad
    update = next_mean / corr_one / (jnp.sqrt(next_var / corr_two) + adam_eps)
    return (param - learn_rate * update, next_mean, next_var)


def spread_columns(slot):
    return jnp.concatenate([slot[0:8], slot[8:16]], axis=1)


def stack_columns(block):
    half = block.shape[1] // 2
    return jnp.concatenate([block[:, :half], block[:, half:]], axis=0)


def exchange_kernel(
    rewards, groups, lengths, hid_in, ups_in, w_in, dn_in, up_in, dm_in, dv_in, um_in, uv_in,
    wb, nd, fu, hig, fdn, fup, fdm, fdv, fum, fuv,
    hid, ups, dn, up, dm, dv, um, uv,
    g, gt, sa, f, a, rx, sy, ty, low,
    cd, cu, nrd, nru, md, mu, frd, fru, hd, hu, sd, su, fd,
    pt, pr1, q, pr2, r, rb, pr3, send_sem, recv_sem, local_sem,
):
    z, yl, x, yh, c = coords()
    slot = 2 * (z // 4) + yl
    count = [0]
    sent = []

    def send(src, dst, off):
        i = count[0]
        count[0] += 1
        assert i < MESSAGES
        copy = pltpu.make_async_remote_copy(
            src_ref=src,
            dst_ref=dst,
            send_sem=send_sem.at[i],
            recv_sem=recv_sem.at[i],
            device_id=device(off),
            device_id_type=MESH,
        )
        copy.start()
        sent.append(copy)
        return copy

    def arrive(copies):
        for copy in copies:
            copy.wait_recv()

    def slot_of(dz, dy):
        return 2 * (((z + dz + 16) % 16) // 4) + (yl + dy) % 2

    def far_send(buf):
        return [send(buf.at[slot], buf.at[slot], off) for off in FAR]

    def far_relay(buf, copies):
        arrive(copies[:2])
        back, ahead = buf.at[slot_of(-4, 0)], buf.at[slot_of(4, 1)]
        return copies[2:] + [send(back, back, PLUS4), send(ahead, ahead, MINUS4)]

    def near_send(buf):
        mine = rows(z % 4, 64)
        low_half, high_half = rows(2 * (z % 4), 32), rows(2 * (z % 4) + 1, 32)
        return [
            send(buf.at[low_half], buf.at[low_half], PLUS2),
            send(buf.at[high_half], buf.at[high_half], MINUS2),
            send(buf.at[mine], buf.at[mine], PLUS1),
            send(buf.at[mine], buf.at[mine], MINUS1),
        ]

    def near_parts(buf, slots):
        across = (z + 2) % 4
        return [
            send(buf.at[rows(2 * across, 32)], slots.at[2, pl.ds(0, 32)], PLUS2),
            send(buf.at[rows(2 * across + 1, 32)], slots.at[2, pl.ds(32, 32)], MINUS2),
            send(buf.at[rows((z + 1) % 4, 64)], slots.at[0], PLUS1),
            send(buf.at[rows((z + 3) % 4, 64)], slots.at[1], MINUS1),
        ]

    def near_sum(buf, slots):
        total = buf[rows(z % 4, 64), :].astype(f32)
        for i in range(3):
            total = total + slots[i].astype(f32)
        return total

    def far_parts(buf, slots):
        relayed = [
            send(buf.at[slot_of(8, 0)], slots.at[5], PLUS4),
            send(buf.at[slot_of(8, 1)], slots.at[6], MINUS4),
        ]
        direct = [
            send(buf.at[slot_of(off[0], off[1])], slots.at[i], off)
            for i, off in enumerate(FAR)
            if i >= 2
        ]
        return relayed, direct

    def relay_parts(buf, slots, held, copies):
        relayed, direct = copies
        for i, off in enumerate(FAR[:2]):
            relayed[i].wait_recv()
            total = buf[slot_of(off[0], off[1])].astype(f32) + slots[5 + i].astype(f32)
            held[i] = total.astype(held.dtype)
            direct.append(send(held.at[i], slots.at[i], off))
        return direct

    def far_sum(buf, slots):
        total = buf[slot].astype(f32)
        for i in range(5):
            total = total + slots[i].astype(f32)
        return total

    def w_rows(zz, half):
        zz = (zz + 16) % 16
        span = rows(yl, 64) if half is None else rows(2 * yl + half, 32)
        return wb.at[zz % 4, zz // 4, span, :]

    def w_send(zz, off, half=None):
        return send(w_rows(zz, half), w_rows(zz, half), off)

    fetches = []
    for i, (src, dst) in enumerate(
        [
            (up_in, up), (dn_in, dn), (w_in, w_rows(z, None)), (ups_in, ups), (hid_in, hid),
            (dm_in, dm), (dv_in, dv), (um_in, um), (uv_in, uv),
        ]
    ):
        fetches.append(pltpu.make_async_copy(src, dst, local_sem.at[i]))
        fetches[-1].start()
    barrier = pltpu.get_barrier_semaphore()
    for off in PEERS:
        pl.semaphore_signal(barrier, inc=1, device_id=device(inverse(off)), device_id_type=MESH)
    fetches[0].wait()
    fetches[1].wait()
    sa[slot, :, 0:512] = stack_columns(up[...]).astype(bf16)
    sa[slot, :, 512:640] = jnp.concatenate([dn[...], jnp.zeros_like(dn[...])], axis=0).astype(bf16)
    pl.semaphore_wait(barrier, len(PEERS))

    far = far_send(sa)
    fetches[2].wait()
    pair_a = [w_send(z, Y_LO)]
    w_far = [w_send(z, PLUS4), w_send(z, MINUS4)]
    for copy in fetches[3:]:
        copy.wait()
    position = lax.broadcasted_iota(jnp.int32, (LEN, 1024), 0)
    for s in range(8):
        total = jnp.float32(0.0)
        for t in range(8):
            total = total + jnp.where(groups[t] == groups[s], rewards[t], jnp.float32(0.0))
        advantage = rewards[s] - total / GROUP
        weight = jnp.where(position < lengths[s], -advantage, jnp.float32(0.0))
        span = slice(LEN * s, LEN * s + LEN)
        g[span, :] = (weight * ups[span, :].astype(f32)).astype(bf16)
    far = far_relay(sa, far)
    gt[...] = jnp.transpose(g[...].astype(f32)).astype(bf16)
    arrive(far)
    for i in range(4):
        pair = jnp.concatenate([sa[2 * i].astype(f32), sa[2 * i + 1].astype(f32)], axis=0)
        block = rows(4 * (z % 4) + i, 16)
        f[block, 0:512] = jnp.concatenate([pair[0:8, 0:512], pair[16:24, 0:512]], 0).astype(bf16)
        f[block, 512:1024] = jnp.concatenate([pair[8:16, 0:512], pair[24:32, 0:512]], 0).astype(bf16)
        f[block, 1024:1152] = jnp.concatenate([pair[0:8, 512:], pair[16:24, 512:]], 0).astype(bf16)
    near = near_send(f)
    arrive(near)

    a[0:256, :] = dot(f[:, 1024:1152], hid[...], 1, 1).astype(bf16)
    a[256:512, :] = dot(f[:, 0:1024], gt[...], 1, 0).astype(bf16)
    j = 2 * x + c
    scattered = []
    for i, off in enumerate(X_CORE):
        to = 2 * ((x + off[2] + 4) % 4) + (c + off[4]) % 2
        scattered.append(send(a.at[rows(to, 64)], rx.at[i], off))
    arrive(w_far)
    w_far2 = [w_send(z - 4, PLUS4, 0), w_send(z + 4, MINUS4, 1)]
    w_near = [w_send(z + b, off) for b in (0, 4, -4) for off in (PLUS1, MINUS1)]
    pair_a += [w_send(z + b, Y_LO) for b in (4, -4)]
    arrive(scattered)
    total = a[rows(j, 64), :].astype(f32)
    for i in range(7):
        total = total + rx[i].astype(f32)
    sy[...] = total.astype(bf16)
    s = send(sy, ty, Y_HI)
    s.wait_recv()
    low[rows(j, 64), :] = (sy[...].astype(f32) + ty[...].astype(f32)).astype(bf16)
    gathered = [send(low.at[rows(j, 64)], low.at[rows(j, 64)], off) for off in X_CORE]
    arrive(w_far2)
    w_near_last = [w_send(z + 8, off) for off in (PLUS1, MINUS1)]
    pair_a.append(w_send(z + 8, Y_LO))
    arrive(gathered)

    cd[...] = (adapter_scale * dot(low[256:512, :], hid[...], 1, 0)).astype(bf16)
    near_d = near_parts(cd, nrd)
    cu[...] = (adapter_scale * dot(low[0:256, :], g[...], 1, 0)).astype(bf16)
    near_u = near_parts(cu, nru)
    arrive(w_near)
    w_near2 = []
    pair_b = []
    for b in (0, 4, -4):
        w_near2 += [w_send(z + 1 + b, MINUS1, 0), w_send(z - 1 + b, PLUS1, 1)]
        pair_a.append(w_send(z + 1 + b, Y_LO))
        pair_b.append(w_send(z - 1 + b, Y_LO))
    arrive(near_d)
    md[...] = near_sum(cd, nrd).reshape(8, 8, 128)
    far_d = far_parts(md, frd)
    arrive(near_u)
    total = near_sum(cu, nru)
    for i in range(8):
        mu[i] = stack_columns(total[8 * i : 8 * i + 8]).astype(bf16)
    far_u = far_parts(mu, fru)
    far_d = relay_parts(md, frd, hd, far_d)
    arrive(w_near_last)
    w_near2 += [w_send(z + 9, MINUS1, 0), w_send(z + 7, PLUS1, 1)]
    pair_a.append(w_send(z + 9, Y_LO))
    pair_b.append(w_send(z + 7, Y_LO))
    far_u = relay_parts(mu, fru, hu, far_u)
    arrive(far_d)
    fdn[...], fdm[...], fdv[...] = adam(dn[...], far_sum(md, frd), dm[...], dv[...])
    sd[slot] = fdn[...]
    far_d = far_send(sd)
    arrive(far_u)
    grad = spread_columns(far_sum(mu, fru))
    fup[...], fum[...], fuv[...] = adam(up[...], grad, um[...], uv[...])
    su[slot] = stack_columns(fup[...]).astype(bf16)
    far_u = far_send(su)
    far_d = far_relay(sd, far_d)
    arrive(w_near2)
    pair_b += [w_send(z + 2 + b, Y_LO) for b in (0, 4, -4, 8)]
    far_u = far_relay(su, far_u)

    flip = (z + c) % 2
    kept = [(z + flip) % 4, (z + flip + 2) % 4]
    sent_on = [(z + 1 - flip) % 4, (z + 3 - flip) % 4]

    def product(step):
        for group in (sent_on[step], kept[step]):
            total = dot(wb[group].reshape(512, 1024), gt[...], 1, 0).astype(bf16)
            pt[group] = total.reshape(4, 128, 256)
            if group is sent_on[step]:
                copy = send(pt.at[group], pr1.at[step], CORE)
        return copy

    def core_sum(step):
        q[step] = (pt[kept[step]].astype(f32) + pr1[step].astype(f32)).astype(bf16)
        return [
            send(q.at[step, (x + off[2] + 4) % 4], pr2.at[step, i], off)
            for i, off in enumerate(X_RING)
        ]

    arrive(pair_a)
    core_a = product(0)
    arrive(far_d)
    fd[rows(z % 4, 64), :] = sd[...].reshape(64, 128).astype(bf16)
    near_d = near_send(fd)
    arrive(far_u)
    for i in range(4):
        pair = jnp.concatenate([su[2 * i].astype(f32), su[2 * i + 1].astype(f32)], axis=0)
        block = rows(4 * (z % 4) + i, 16)
        fu[block, 0:512] = jnp.concatenate([pair[0:8], pair[16:24]], 0).astype(bf16)
        fu[block, 512:1024] = jnp.concatenate([pair[8:16], pair[24:32]], 0).astype(bf16)
    near_u = near_send(fu)
    arrive([core_a])
    x_parts = core_sum(0)

    k = 2 * x + yh
    arrive(near_d)
    nd[c, k] = jnp.transpose(fd[...].astype(f32)).astype(bf16)
    s = send(nd.at[c, k], nd.at[c, k], Y_HI)
    arrive(pair_b)
    core_b = product(1)
    s.wait_recv()
    spread = [send(nd.at[c, rows(x, 2)], nd.at[c, rows(x, 2)], off) for off in X_RING]
    arrive([core_b])
    x_parts += core_sum(1)
    arrive(spread)
    s = send(nd.at[c], nd.at[c], CORE)
    arrive(x_parts)
    for step in range(2):
        total = q[step, x].astype(f32)
        for i in range(3):
            total = total + pr2[step, i].astype(f32)
        r[step] = total
    mine = (kept[0] // 2 + yh) % 2
    rb[...] = r[1 - mine].astype(bf16)
    s_p = send(rb, pr3, Y_HI)
    own = adapter_scale * dot(low[256:512, :], f[:, 1024:1152], 0, 0)
    s_p.wait_recv()
    hig[...] = (jnp.transpose(r[mine] + pr3[...].astype(f32)) + own).astype(bf16)
    s.wait_recv()
    arrive(near_u)
    for copy in sent:
        copy.wait_send()


def exchange(*args):
    def out(shape, dtype):
        return jax.ShapeDtypeStruct(shape, dtype)

    vmem = pl.BlockSpec(memory_space=pltpu.VMEM)
    scratch = [
        ((256, 128), bf16), ((256, 1024), bf16), ((8, 128), f32), ((8, 1024), f32),
        ((8, 128), f32), ((8, 128), f32), ((8, 1024), f32), ((8, 1024), f32),
        ((256, 1024), bf16), ((1024, 256), bf16), ((8, 16, 640), bf16), ((256, 1152), bf16),
        ((512, 256), bf16), ((7, 64, 256), bf16), ((64, 256), bf16), ((64, 256), bf16),
        ((512, 256), bf16),
        ((256, 128), bf16), ((256, 1024), bf16), ((3, 64, 128), bf16), ((3, 64, 1024), bf16),
        ((8, 8, 128), f32), ((8, 16, 512), bf16), ((7, 8, 128), f32), ((7, 16, 512), bf16),
        ((2, 8, 128), f32), ((2, 16, 512), bf16),
        ((8, 8, 128), f32), ((8, 16, 512), bf16), ((256, 128), bf16),
        ((4, 4, 128, 256), bf16), ((2, 4, 128, 256), bf16), ((2, 4, 128, 256), bf16),
        ((2, 3, 128, 256), bf16), ((2, 128, 256), f32), ((128, 256), bf16), ((128, 256), bf16),
    ]
    return pl.pallas_call(
        exchange_kernel,
        name="exchange",
        out_shape=[
            out((4, 4, 128, 1024), bf16),
            out((2, 8, 128, 256), bf16),
            out((256, 1024), bf16),
            out((256, 128), bf16),
            out((8, 128), f32),
            out((8, 1024), f32),
            out((8, 128), f32),
            out((8, 128), f32),
            out((8, 1024), f32),
            out((8, 1024), f32),
        ],
        in_specs=[pl.BlockSpec(memory_space=pltpu.SMEM)] * 3
        + [pl.BlockSpec(memory_space=pltpu.HBM)] * 9,
        out_specs=[vmem] * 10,
        scratch_shapes=[pltpu.VMEM(shape, dtype) for shape, dtype in scratch]
        + [
            pltpu.SemaphoreType.DMA((MESSAGES,)),
            pltpu.SemaphoreType.DMA((MESSAGES,)),
            pltpu.SemaphoreType.DMA((9,)),
        ],
        compiler_params=pltpu.CompilerParams(
            collective_id=0, has_side_effects=True, vmem_limit_bytes=62 << 20
        ),
    )(*args)


def merge_kernel(w, nd, fu, *refs):
    merged = refs[-1]
    i = pl.program_id(0)
    factor = jnp.concatenate([nd[n % 2, 2 * i + n // 2] for n in range(4)], axis=0)
    delta = adapter_scale * dot(factor, fu[...], 1, 0)
    for n in range(4):
        span = slice(128 * n, 128 * n + 128)
        merged[span, :] = (w[n, i].astype(f32) + delta[span]).astype(bf16)

    @pl.when(i == 0)
    def _():
        for n in range(7):
            refs[7 + n][...] = refs[n][...]


def merge(w, nd, fu, *rest):
    vmem = pl.BlockSpec(memory_space=pltpu.VMEM)

    def whole(array):
        return pl.BlockSpec(array.shape, lambda i: (0,) * len(array.shape))

    return pl.pallas_call(
        merge_kernel,
        name="merge",
        grid=(4,),
        in_specs=[vmem] * 10,
        out_specs=[whole(array) for array in rest]
        + [pl.BlockSpec((512, 1024), lambda i: (i, 0))],
        out_shape=[jax.ShapeDtypeStruct(array.shape, array.dtype) for array in rest]
        + [jax.ShapeDtypeStruct((2048, 1024), bf16)],
        compiler_params=pltpu.CompilerParams(vmem_limit_bytes=62 << 20),
    )(w, nd, fu, *rest)


def body(
    hidden,
    upstream,
    rewards,
    groups,
    lengths,
    frozen_projection_weight,
    *adapter,
):
    w_all, nd, fu, *rest = exchange(
        rewards, groups, lengths, hidden, upstream, frozen_projection_weight, *adapter
    )
    return tuple(merge(w_all, nd, fu, *rest))


def solution(mesh):
    split = P("dp", "fsdp")
    in_specs = (split, split, P("dp"), P("dp"), P("dp")) + (split,) * 7
    out_specs = (split,) * 7 + (P(None, "fsdp"),)
    return jax.shard_map(body, mesh=mesh, in_specs=in_specs, out_specs=out_specs, check_vma=False)
```

time: 169 us -> 125 us (0.74)
  Pallas kernels: 158 us -> 123 us
  local copies, waits for them, and re-layouts: 7.24 us -> 0 us
  other arithmetic: 2.3 us -> 0 us
    pallas_call x2, Pallas kernels: 158 us -> 123 us  [the longest x1 117 us: exchange(): pl.pallas_call(exchange_kernel, name='exchange', out_shape=[out((4, 4, 12...]
    unnamed x18 -> x0, local copies, waits for them, and re-layouts: 7.11 us -> none
where the time goes in v2:
time: 125 us; the launch traced here: 124 us
  Pallas kernels  123 us (98%)
    pallas_call x1, Pallas kernels, exchange(): pl.pallas_call(exchange_kernel, name='exchange', out_shape=[out((4, 4, 12...  117 us
    pallas_call x1, Pallas kernels, merge(): pl.pallas_call(merge_kernel, name='merge', grid=(4,), in_specs=[vmem] * 1...  6.14 us

profile of v2, /device:TPU:1, one launch (start us, length us, event | category | flops | bytes accessed | tf_op | source)
XLA Modules:
  0.0 124.0 jit_solution(14088555425838910597)
XLA Ops:
  0.6 117.2 %exchange.1 = (bf16[4,4,128,1024]{3,2,1,0:T(8,128)(2,1)}, bf16[2,8,128,256]{3,2,1,0:T(8,128)(2,1)}, bf16[256,1024]{1,0:T(8,128)(2,1)}, bf16[256,128]{1,0:T(8,128...) custom-call(f32[8]{0:T(128)} %rewards.1, ...), custom_call_target="tpu_custom_call" | custom-call | tf_op jit(solution)/shard_map/exchange/pallas_call | solution.py:377
  117.9 6.1 %merge.1 = (bf16[256,128]{1,0:T(8,128)(2,1)}, f32[8,128]{1,0:T(8,128)}, f32[8,1024]{1,0:T(8,128)}, f32[8,128]{1,0:T(8,128)}, f32[8,128]{1,0:T(8,128)}, /*index=5...) custom-call(bf16[4,4,128,1024]{3,2,1,0:T(8,128)(2,1)} %get-tuple-element.18.w, ...), custom_call_target="tpu_custom_call" | custom-call | tf_op jit(solution)/shard_map/merge/pallas_call | solution.py:428

commit v3 on v2

--- a/solution.py
+++ b/solution.py
@@ -81,9 +81,9 @@
 
 def exchange_kernel(
     rewards, groups, lengths, hid_in, ups_in, w_in, dn_in, up_in, dm_in, dv_in, um_in, uv_in,
-    wb, nd, fu, hig, fdn, fup, fdm, fdv, fum, fuv,
+    w_all, nd, fu, hig, fdn, fup, fdm, fdv, fum, fuv,
     hid, ups, dn, up, dm, dv, um, uv,
-    g, gt, sa, f, a, rx, sy, ty, low,
+    wb, g, gt, sa, f, a, rx, sy, ty, low,
     cd, cu, nrd, nru, md, mu, frd, fru, hd, hu, sd, su, fd,
     pt, pr1, q, pr2, r, rb, pr3, send_sem, recv_sem, local_sem,
 ):
@@ -183,6 +183,22 @@
     def w_send(zz, off, half=None):
         return send(w_rows(zz, half), w_rows(zz, half), off)
 
+    def w_step(step):
+        arrive(w_ring)
+        w_ring.clear()
+        if step < 9:
+            half = (0, 1) if step == 8 else (None, None)
+            w_ring.extend(
+                [w_send(z + 1 - step, PLUS1, half[0]), w_send(z - 1 + step, MINUS1, half[1])]
+            )
+        w_ready.extend([z] if step == 1 else [z + 8] if step == 9 else [z + 1 - step, z - 1 + step])
+        if step != 4:
+            w_pair.extend([w_send(zz, Y_LO) for zz in w_ready])
+            w_ready.clear()
+
+    w_ring = []
+    w_ready = []
+    w_pair = []
     fetches = []
     for i, (src, dst) in enumerate(
         [
@@ -192,6 +208,26 @@
     ):
         fetches.append(pltpu.make_async_copy(src, dst, local_sem.at[i]))
         fetches[-1].start()
+    flip = (z + c) % 2
+    kept = [(z + flip) % 4, (z + flip + 2) % 4]
+    sent_on = [(z + 1 - flip) % 4, (z + 3 - flip) % 4]
+
+    def product(step):
+        for group in (sent_on[step], kept[step]):
+            total = dot(wb[group].reshape(512, 1024), gt[...], 1, 0).astype(bf16)
+            pt[group] = total.reshape(4, 128, 256)
+            if group is sent_on[step]:
+                copy = send(pt.at[group], pr1.at[step], CORE)
+        return copy
+
+    def core_sum(step):
+        q[step] = (pt[kept[step]].astype(f32) + pr1[step].astype(f32)).astype(bf16)
+        return [
+            send(q.at[step, (x + off[2] + 4) % 4], pr2.at[step, i], off)
+            for i, off in enumerate(X_RING)
+        ]
+
+
     barrier = pltpu.get_barrier_semaphore()
     for off in PEERS:
         pl.semaphore_signal(barrier, inc=1, device_id=device(inverse(off)), device_id_type=MESH)
@@ -203,8 +239,7 @@
 
     far = far_send(sa)
     fetches[2].wait()
-    pair_a = [w_send(z, Y_LO)]
-    w_far = [w_send(z, PLUS4), w_send(z, MINUS4)]
+    w_step(1)
     for copy in fetches[3:]:
         copy.wait()
     position = lax.broadcasted_iota(jnp.int32, (LEN, 1024), 0)
@@ -226,6 +261,7 @@
         f[block, 512:1024] = jnp.concatenate([pair[8:16, 0:512], pair[24:32, 0:512]], 0).astype(bf16)
         f[block, 1024:1152] = jnp.concatenate([pair[0:8, 512:], pair[16:24, 512:]], 0).astype(bf16)
     near = near_send(f)
+    w_step(2)
     arrive(near)
 
     a[0:256, :] = dot(f[:, 1024:1152], hid[...], 1, 1).astype(bf16)
@@ -235,87 +271,64 @@
     for i, off in enumerate(X_CORE):
         to = 2 * ((x + off[2] + 4) % 4) + (c + off[4]) % 2
         scattered.append(send(a.at[rows(to, 64)], rx.at[i], off))
-    arrive(w_far)
-    w_far2 = [w_send(z - 4, PLUS4, 0), w_send(z + 4, MINUS4, 1)]
-    w_near = [w_send(z + b, off) for b in (0, 4, -4) for off in (PLUS1, MINUS1)]
-    pair_a += [w_send(z + b, Y_LO) for b in (4, -4)]
-    arrive(scattered)
+    w_step(3)
+    arrive(scattered[:4])
+    w_step(4)
+    arrive(scattered[4:])
     total = a[rows(j, 64), :].astype(f32)
     for i in range(7):
         total = total + rx[i].astype(f32)
     sy[...] = total.astype(bf16)
     s = send(sy, ty, Y_HI)
+    w_step(5)
     s.wait_recv()
     low[rows(j, 64), :] = (sy[...].astype(f32) + ty[...].astype(f32)).astype(bf16)
     gathered = [send(low.at[rows(j, 64)], low.at[rows(j, 64)], off) for off in X_CORE]
-    arrive(w_far2)
-    w_near_last = [w_send(z + 8, off) for off in (PLUS1, MINUS1)]
-    pair_a.append(w_send(z + 8, Y_LO))
+    w_step(6)
     arrive(gathered)
 
     cd[...] = (adapter_scale * dot(low[256:512, :], hid[...], 1, 0)).astype(bf16)
     near_d = near_parts(cd, nrd)
     cu[...] = (adapter_scale * dot(low[0:256, :], g[...], 1, 0)).astype(bf16)
     near_u = near_parts(cu, nru)
-    arrive(w_near)
-    w_near2 = []
-    pair_b = []
-    for b in (0, 4, -4):
-        w_near2 += [w_send(z + 1 + b, MINUS1, 0), w_send(z - 1 + b, PLUS1, 1)]
-        pair_a.append(w_send(z + 1 + b, Y_LO))
-        pair_b.append(w_send(z - 1 + b, Y_LO))
+    w_step(7)
     arrive(near_d)
     md[...] = near_sum(cd, nrd).reshape(8, 8, 128)
     far_d = far_parts(md, frd)
+    w_step(8)
+    far_d = relay_parts(md, frd, hd, far_d)
     arrive(near_u)
     total = near_sum(cu, nru)
     for i in range(8):
         mu[i] = stack_columns(total[8 * i : 8 * i + 8]).astype(bf16)
     far_u = far_parts(mu, fru)
-    far_d = relay_parts(md, frd, hd, far_d)
-    arrive(w_near_last)
-    w_near2 += [w_send(z + 9, MINUS1, 0), w_send(z + 7, PLUS1, 1)]
-    pair_a.append(w_send(z + 9, Y_LO))
-    pair_b.append(w_send(z + 7, Y_LO))
-    far_u = relay_parts(mu, fru, hu, far_u)
+    w_step(9)
     arrive(far_d)
     fdn[...], fdm[...], fdv[...] = adam(dn[...], far_sum(md, frd), dm[...], dv[...])
     sd[slot] = fdn[...]
     far_d = far_send(sd)
+    far_u = relay_parts(mu, fru, hu, far_u)
+    far_d = far_relay(sd, far_d)
     arrive(far_u)
     grad = spread_columns(far_sum(mu, fru))
     fup[...], fum[...], fuv[...] = adam(up[...], grad, um[...], uv[...])
     su[slot] = stack_columns(fup[...]).astype(bf16)
     far_u = far_send(su)
-    far_d = far_relay(sd, far_d)
-    arrive(w_near2)
-    pair_b += [w_send(z + 2 + b, Y_LO) for b in (0, 4, -4, 8)]
-    far_u = far_relay(su, far_u)
-
-    flip = (z + c) % 2
-    kept = [(z + flip) % 4, (z + flip + 2) % 4]
-    sent_on = [(z + 1 - flip) % 4, (z + 3 - flip) % 4]
-
-    def product(step):
-        for group in (sent_on[step], kept[step]):
-            total = dot(wb[group].reshape(512, 1024), gt[...], 1, 0).astype(bf16)
-            pt[group] = total.reshape(4, 128, 256)
-            if group is sent_on[step]:
-                copy = send(pt.at[group], pr1.at[step], CORE)
-        return copy
-
-    def core_sum(step):
-        q[step] = (pt[kept[step]].astype(f32) + pr1[step].astype(f32)).astype(bf16)
-        return [
-            send(q.at[step, (x + off[2] + 4) % 4], pr2.at[step, i], off)
-            for i, off in enumerate(X_RING)
-        ]
-
-    arrive(pair_a)
-    core_a = product(0)
+    arrive(w_pair)
+    w_copy = pltpu.make_async_copy(wb, w_all, local_sem.at[9])
+    w_copy.start()
+    core = [product(0), product(1)]
     arrive(far_d)
     fd[rows(z % 4, 64), :] = sd[...].reshape(64, 128).astype(bf16)
     near_d = near_send(fd)
+    far_u = far_relay(su, far_u)
+    arrive(core)
+    x_parts = core_sum(0) + core_sum(1)
+
+    k = 2 * x + yh
+    arrive(near_d)
+    nd[c, k] = jnp.transpose(fd[...].astype(f32)).astype(bf16)
+    s = send(nd.at[c, k], nd.at[c, k], Y_HI)
     arrive(far_u)
     for i in range(4):
         pair = jnp.concatenate([su[2 * i].astype(f32), su[2 * i + 1].astype(f32)], axis=0)
@@ -323,21 +336,8 @@
         fu[block, 0:512] = jnp.concatenate([pair[0:8], pair[16:24]], 0).astype(bf16)
         fu[block, 512:1024] = jnp.concatenate([pair[8:16], pair[24:32]], 0).astype(bf16)
     near_u = near_send(fu)
-    arrive([core_a])
-    x_parts = core_sum(0)
-
-    k = 2 * x + yh
-    arrive(near_d)
-    nd[c, k] = jnp.transpose(fd[...].astype(f32)).astype(bf16)
-    s = send(nd.at[c, k], nd.at[c, k], Y_HI)
-    arrive(pair_b)
-    core_b = product(1)
     s.wait_recv()
     spread = [send(nd.at[c, rows(x, 2)], nd.at[c, rows(x, 2)], off) for off in X_RING]
-    arrive([core_b])
-    x_parts += core_sum(1)
-    arrive(spread)
-    s = send(nd.at[c], nd.at[c], CORE)
     arrive(x_parts)
     for step in range(2):
         total = q[step, x].astype(f32)
@@ -350,10 +350,13 @@
     own = adapter_scale * dot(low[256:512, :], f[:, 1024:1152], 0, 0)
     s_p.wait_recv()
     hig[...] = (jnp.transpose(r[mine] + pr3[...].astype(f32)) + own).astype(bf16)
+    arrive(spread)
+    s = send(nd.at[c], nd.at[c], CORE)
     s.wait_recv()
     arrive(near_u)
     for copy in sent:
         copy.wait_send()
+    w_copy.wait()
 
 
 def exchange(*args):
@@ -364,6 +367,7 @@
     scratch = [
         ((256, 128), bf16), ((256, 1024), bf16), ((8, 128), f32), ((8, 1024), f32),
         ((8, 128), f32), ((8, 128), f32), ((8, 1024), f32), ((8, 1024), f32),
+        ((4, 4, 128, 1024), bf16),
         ((256, 1024), bf16), ((1024, 256), bf16), ((8, 16, 640), bf16), ((256, 1152), bf16),
         ((512, 256), bf16), ((7, 64, 256), bf16), ((64, 256), bf16), ((64, 256), bf16),
         ((512, 256), bf16),
@@ -391,12 +395,12 @@
         ],
         in_specs=[pl.BlockSpec(memory_space=pltpu.SMEM)] * 3
         + [pl.BlockSpec(memory_space=pltpu.HBM)] * 9,
-        out_specs=[vmem] * 10,
+        out_specs=[pl.BlockSpec(memory_space=pltpu.HBM)] + [vmem] * 9,
         scratch_shapes=[pltpu.VMEM(shape, dtype) for shape, dtype in scratch]
         + [
             pltpu.SemaphoreType.DMA((MESSAGES,)),
             pltpu.SemaphoreType.DMA((MESSAGES,)),
-            pltpu.SemaphoreType.DMA((9,)),
+            pltpu.SemaphoreType.DMA((10,)),
         ],
         compiler_params=pltpu.CompilerParams(
             collective_id=0, has_side_effects=True, vmem_limit_bytes=62 << 20
@@ -407,11 +411,12 @@
 def merge_kernel(w, nd, fu, *refs):
     merged = refs[-1]
     i = pl.program_id(0)
-    factor = jnp.concatenate([nd[n % 2, 2 * i + n // 2] for n in range(4)], axis=0)
+    blocks = [(n, half) for half in range(2) for n in range(4)]
+    factor = jnp.concatenate([nd[n % 2, 2 * half + n // 2] for n, half in blocks], axis=0)
     delta = adapter_scale * dot(factor, fu[...], 1, 0)
-    for n in range(4):
-        span = slice(128 * n, 128 * n + 128)
-        merged[span, :] = (w[n, i].astype(f32) + delta[span]).astype(bf16)
+    for at, (n, half) in enumerate(blocks):
+        span = slice(128 * at, 128 * at + 128)
+        merged[span, :] = (w[n, half].astype(f32) + delta[span]).astype(bf16)
 
     @pl.when(i == 0)
     def _():
@@ -420,18 +425,21 @@
 
 
 def merge(w, nd, fu, *rest):
-    vmem = pl.BlockSpec(memory_space=pltpu.VMEM)
-
     def whole(array):
         return pl.BlockSpec(array.shape, lambda i: (0,) * len(array.shape))
 
     return pl.pallas_call(
         merge_kernel,
         name="merge",
-        grid=(4,),
-        in_specs=[vmem] * 10,
+        grid=(2,),
+        in_specs=[
+            pl.BlockSpec((4, 2, 128, 1024), lambda i: (0, i, 0, 0)),
+            pl.BlockSpec((2, 4, 128, 256), lambda i: (0, i, 0, 0)),
+            whole(fu),
+        ]
+        + [whole(array) for array in rest],
         out_specs=[whole(array) for array in rest]
-        + [pl.BlockSpec((512, 1024), lambda i: (i, 0))],
+        + [pl.BlockSpec((1024, 1024), lambda i: (i, 0))],
         out_shape=[jax.ShapeDtypeStruct(array.shape, array.dtype) for array in rest]
         + [jax.ShapeDtypeStruct((2048, 1024), bf16)],
         compiler_params=pltpu.CompilerParams(vmem_limit_bytes=62 << 20),

time: 125 us -> 109 us (0.87)
  Pallas kernels: 123 us -> 108 us
    pallas_call x1, Pallas kernels: 117 us -> 104 us  [exchange(): pl.pallas_call(exchange_kernel, name='exchange', out_shape=[out((4, 4, 12...]
    pallas_call x1, Pallas kernels: 6.14 us -> 4.82 us  [merge(): pl.pallas_call(merge_kernel, name='merge', grid=(2,), in_specs=[pl.BlockS...]
where the time goes in v3:
time: 109 us
  Pallas kernels  108 us (99%)
    pallas_call x1, Pallas kernels, exchange(): pl.pallas_call(exchange_kernel, name='exchange', out_shape=[out((4, 4, 12...  104 us
    pallas_call x1, Pallas kernels, merge(): pl.pallas_call(merge_kernel, name='merge', grid=(2,), in_specs=[pl.BlockS...  4.82 us

profile of v3, /device:TPU:1, one launch (start us, length us, event | category | flops | bytes accessed | tf_op | source)
XLA Modules:
  0.0 109.1 jit_solution(4293682630326095509)
XLA Ops:
  0.6 103.6 %exchange.1 = (bf16[4,4,128,1024]{3,2,1,0:T(8,128)(2,1)}, bf16[2,8,128,256]{3,2,1,0:T(8,128)(2,1)}, bf16[256,1024]{1,0:T(8,128)(2,1)}, bf16[256,128]{1,0:T(8,128...) custom-call(f32[8]{0:T(128)} %rewards.1, ...), custom_call_target="tpu_custom_call" | custom-call | tf_op jit(solution)/shard_map/exchange/pallas_call | solution.py:381
  104.3 4.8 %merge.1 = (bf16[256,128]{1,0:T(8,128)(2,1)}, f32[8,128]{1,0:T(8,128)}, f32[8,1024]{1,0:T(8,128)}, f32[8,128]{1,0:T(8,128)}, f32[8,128]{1,0:T(8,128)}, /*index=5...) custom-call(bf16[4,4,128,1024]{3,2,1,0:T(8,128)(2,1)} %get-tuple-element.18.w, ...), custom_call_target="tpu_custom_call" | custom-call | tf_op jit(solution)/shard_map/merge/pallas_call | solution.py:431

commit v4 on v3

--- a/solution.py
+++ b/solution.py
@@ -295,20 +295,20 @@
     arrive(near_d)
     md[...] = near_sum(cd, nrd).reshape(8, 8, 128)
     far_d = far_parts(md, frd)
-    w_step(8)
     far_d = relay_parts(md, frd, hd, far_d)
     arrive(near_u)
     total = near_sum(cu, nru)
     for i in range(8):
         mu[i] = stack_columns(total[8 * i : 8 * i + 8]).astype(bf16)
     far_u = far_parts(mu, fru)
-    w_step(9)
+    w_step(8)
     arrive(far_d)
     fdn[...], fdm[...], fdv[...] = adam(dn[...], far_sum(md, frd), dm[...], dv[...])
     sd[slot] = fdn[...]
     far_d = far_send(sd)
     far_u = relay_parts(mu, fru, hu, far_u)
     far_d = far_relay(sd, far_d)
+    w_step(9)
     arrive(far_u)
     grad = spread_columns(far_sum(mu, fru))
     fup[...], fum[...], fuv[...] = adam(up[...], grad, um[...], uv[...])
@@ -337,7 +337,9 @@
         fu[block, 512:1024] = jnp.concatenate([pair[8:16], pair[24:32]], 0).astype(bf16)
     near_u = near_send(fu)
     s.wait_recv()
-    spread = [send(nd.at[c, rows(x, 2)], nd.at[c, rows(x, 2)], off) for off in X_RING]
+    block = nd.at[c, rows(x, 2)]
+    spread = [send(block, block, off) for off in X_RING]
+    across = [send(block, block, CORE)]
     arrive(x_parts)
     for step in range(2):
         total = q[step, x].astype(f32)
@@ -348,11 +350,13 @@
     rb[...] = r[1 - mine].astype(bf16)
     s_p = send(rb, pr3, Y_HI)
     own = adapter_scale * dot(low[256:512, :], f[:, 1024:1152], 0, 0)
+    for i in (1, 2, 0):
+        arrive([spread[i]])
+        block = nd.at[c, rows((x - X_RING[i][2] + 4) % 4, 2)]
+        across.append(send(block, block, CORE))
     s_p.wait_recv()
     hig[...] = (jnp.transpose(r[mine] + pr3[...].astype(f32)) + own).astype(bf16)
-    arrive(spread)
-    s = send(nd.at[c], nd.at[c], CORE)
-    s.wait_recv()
+    arrive(across)
     arrive(near_u)
     for copy in sent:
         copy.wait_send()

time: 109 us -> 109 us (level)
  no operation moved by 1% of the time
where the time goes in v4:
time: 109 us
  Pallas kernels  109 us (100%)
    pallas_call x1, Pallas kernels, exchange(): pl.pallas_call(exchange_kernel, name='exchange', out_shape=[out((4, 4, 12...  104 us
    pallas_call x1, Pallas kernels, merge(): pl.pallas_call(merge_kernel, name='merge', grid=(2,), in_specs=[pl.BlockS...  4.82 us

profile of v4, /device:TPU:1, one launch (start us, length us, event | category | flops | bytes accessed | tf_op | source)
XLA Modules:
  0.0 109.2 jit_solution(11629291285231398853)
XLA Ops:
  0.6 103.7 %exchange.1 = (bf16[4,4,128,1024]{3,2,1,0:T(8,128)(2,1)}, bf16[2,8,128,256]{3,2,1,0:T(8,128)(2,1)}, bf16[256,1024]{1,0:T(8,128)(2,1)}, bf16[256,128]{1,0:T(8,128...) custom-call(f32[8]{0:T(128)} %rewards.1, ...), custom_call_target="tpu_custom_call" | custom-call | tf_op jit(solution)/shard_map/exchange/pallas_call | solution.py:385
  104.3 4.8 %merge.1 = (bf16[256,128]{1,0:T(8,128)(2,1)}, f32[8,128]{1,0:T(8,128)}, f32[8,1024]{1,0:T(8,128)}, f32[8,128]{1,0:T(8,128)}, f32[8,128]{1,0:T(8,128)}, /*index=5...) custom-call(bf16[4,4,128,1024]{3,2,1,0:T(8,128)(2,1)} %get-tuple-element.18.w, ...), custom_call_target="tpu_custom_call" | custom-call | tf_op jit(solution)/shard_map/merge/pallas_call | solution.py:435

commit v5 on v4

--- a/solution.py
+++ b/solution.py
@@ -192,9 +192,8 @@
                 [w_send(z + 1 - step, PLUS1, half[0]), w_send(z - 1 + step, MINUS1, half[1])]
             )
         w_ready.extend([z] if step == 1 else [z + 8] if step == 9 else [z + 1 - step, z - 1 + step])
-        if step != 4:
-            w_pair.extend([w_send(zz, Y_LO) for zz in w_ready])
-            w_ready.clear()
+        w_pair.extend([w_send(zz, Y_LO) for zz in w_ready])
+        w_ready.clear()
 
     w_ring = []
     w_ready = []
@@ -253,6 +252,7 @@
         g[span, :] = (weight * ups[span, :].astype(f32)).astype(bf16)
     far = far_relay(sa, far)
     gt[...] = jnp.transpose(g[...].astype(f32)).astype(bf16)
+    w_step(2)
     arrive(far)
     for i in range(4):
         pair = jnp.concatenate([sa[2 * i].astype(f32), sa[2 * i + 1].astype(f32)], axis=0)
@@ -261,7 +261,7 @@
         f[block, 512:1024] = jnp.concatenate([pair[8:16, 0:512], pair[24:32, 0:512]], 0).astype(bf16)
         f[block, 1024:1152] = jnp.concatenate([pair[0:8, 512:], pair[16:24, 512:]], 0).astype(bf16)
     near = near_send(f)
-    w_step(2)
+    w_step(3)
     arrive(near)
 
     a[0:256, :] = dot(f[:, 1024:1152], hid[...], 1, 1).astype(bf16)
@@ -271,10 +271,8 @@
     for i, off in enumerate(X_CORE):
         to = 2 * ((x + off[2] + 4) % 4) + (c + off[4]) % 2
         scattered.append(send(a.at[rows(to, 64)], rx.at[i], off))
-    w_step(3)
-    arrive(scattered[:4])
     w_step(4)
-    arrive(scattered[4:])
+    arrive(scattered)
     total = a[rows(j, 64), :].astype(f32)
     for i in range(7):
         total = total + rx[i].astype(f32)

time: 109 us -> 109 us (level)
  no operation moved by 1% of the time
where the time goes in v5:
time: 109 us; the launch traced here: 108 us
  Pallas kernels  108 us (99%)
    pallas_call x1, Pallas kernels, exchange(): pl.pallas_call(exchange_kernel, name='exchange', out_shape=[out((4, 4, 12...  103 us
    pallas_call x1, Pallas kernels, merge(): pl.pallas_call(merge_kernel, name='merge', grid=(2,), in_specs=[pl.BlockS...  4.82 us

profile of v5, /device:TPU:1, one launch (start us, length us, event | category | flops | bytes accessed | tf_op | source)
XLA Modules:
  0.0 108.4 jit_solution(8802775638944663092)
XLA Ops:
  0.6 103.0 %exchange.1 = (bf16[4,4,128,1024]{3,2,1,0:T(8,128)(2,1)}, bf16[2,8,128,256]{3,2,1,0:T(8,128)(2,1)}, bf16[256,1024]{1,0:T(8,128)(2,1)}, bf16[256,128]{1,0:T(8,128...) custom-call(f32[8]{0:T(128)} %rewards.1, ...), custom_call_target="tpu_custom_call" | custom-call | tf_op jit(solution)/shard_map/exchange/pallas_call | solution.py:383
  103.6 4.8 %merge.1 = (bf16[256,128]{1,0:T(8,128)(2,1)}, f32[8,128]{1,0:T(8,128)}, f32[8,1024]{1,0:T(8,128)}, f32[8,128]{1,0:T(8,128)}, f32[8,128]{1,0:T(8,128)}, /*index=5...) custom-call(bf16[4,4,128,1024]{3,2,1,0:T(8,128)(2,1)} %get-tuple-element.18.w, ...), custom_call_target="tpu_custom_call" | custom-call | tf_op jit(solution)/shard_map/merge/pallas_call | solution.py:433
